TPU v7x, 32 devices: a whole 2x2x4 slice. The times are simulated.
32 devices in a mesh: groups: 2 (over y), coord: 8 (over z, x), ckpt: 2 (over core).
Axes of the slice: x: 2, y: 2, z: 4, core: 2. Of those that a mesh axis runs over, the one named last changes fastest.
Arguments:
- projection_input: bfloat16 [2, 2, 384, 4096], P('ckpt', 'groups', None, 'coord'), parts along dimension 1, may hold values from -6 to 6
- gate_output_gradient: bfloat16 [2, 2, 14336, 384], P('ckpt', 'groups', 'coord'), parts along dimension 1, may hold values from -0.59765625 to 0.59765625
- up_output_gradient: bfloat16 [2, 2, 14336, 384], P('ckpt', 'groups', 'coord'), parts along dimension 1, may hold values from -0.59765625 to 0.59765625
- hidden: bfloat16 [2, 2, 14336, 384], P('ckpt', 'groups', 'coord'), parts along dimension 1, may hold values from -6 to 6
- down_output_gradient: bfloat16 [2, 2, 384, 4096], P('ckpt', 'groups', None, 'coord'), parts along dimension 1, may hold values from -0.59765625 to 0.59765625
- gate_adapter_first: bfloat16 [2, 4096, 128], P('ckpt', 'coord'), may hold values from -0.09375 to 0.09375
- gate_adapter_second: bfloat16 [2, 14336, 128], P('ckpt', 'coord'), may hold values from -0.5 to 0.5
- up_adapter_first: bfloat16 [2, 4096, 128], P('ckpt', 'coord'), may hold values from -0.09375 to 0.09375
- up_adapter_second: bfloat16 [2, 14336, 128], P('ckpt', 'coord'), may hold values from -0.5 to 0.5
- down_adapter_first: bfloat16 [2, 14336, 128], P('ckpt', 'coord'), may hold values from -0.046875 to 0.046875
- down_adapter_second: bfloat16 [2, 4096, 128], P('ckpt', 'coord'), may hold values from -0.5 to 0.5
- random_sign_flags: int32 [16777216], P(('coord', 'ckpt')), may hold values 0 or 1
- sampled_coordinate_index: int32 [8192], replicated, may hold values from 0 to 16777215
Outputs:
- features: float32 [2, 8192], P('groups'), parts along dimension 0
There are 2 independent parts, one for each index of `groups`. A program takes and returns all parts, laid end to end along the dimension named above; an argument that names none is the same for every part. Nothing has to cross between parts.
All inputs are finite; a program needn't handle non-finite values. No bound on the sum of `random_sign_flags` on one device may be relied on, other than what follows from the above.
Results may differ from a plain program's by a relative error of at most 0.0031.
Values may be sent and summed in bfloat16 or wider, within the bound.
No kernel may reach another device: no remote copies, remote signals or barrier semaphores. Data moves between devices by JAX's collectives and lax.ppermute only.
A program may use at most 64 MiB of HBM per device.

v0:
```python
import functools

import jax
import jax.numpy as jnp
from jax import lax
from jax.experimental import pallas as pl
from jax.experimental.pallas import tpu as pltpu
from jax.sharding import PartitionSpec as P

F32 = jnp.float32
BF16 = jnp.bfloat16
MIB = 2**20
adapter_scale = 2.0

ANY = pl.BlockSpec(memory_space=pl.ANY)
VMEM = pl.BlockSpec(memory_space=pltpu.VMEM)
SMEM = pl.BlockSpec(memory_space=pltpu.SMEM)


def limit(size):
    return pltpu.CompilerParams(vmem_limit_bytes=int(size * MIB))


def in_hbm(value):
    return pltpu.with_memory_space_constraint(value, pltpu.HBM)


def exchange(value, axis, apart):
    pairs = [(source, source ^ apart) for source in range(lax.axis_size(axis))]
    return lax.ppermute(value, axis, pairs)


def dot(left, right, contract):
    return lax.dot_general(left, right, (contract, ((), ())), preferred_element_type=F32)


def fetch(sources, targets, sems, cuts):
    groups = []
    slot = 0
    for source, target, cut in zip(sources, targets, cuts, strict=True):
        rows = source.shape[0]
        size = -(-rows // (cut * 16)) * 16
        group = []
        for begin in range(0, rows, size):
            end = min(begin + size, rows)
            copy = pltpu.make_async_copy(
                source.at[begin:end], target.at[begin:end], sems.at[slot]
            )
            copy.start()
            group.append(copy)
            slot += 1
        groups.append(group)

    def wait(which):
        for copy in groups[which]:
            copy.wait()

    return wait


def stages_of(count):
    stages, shift = [], 0
    while count > 1:
        radix = 2 if shift == 0 else min(4, count)
        stages.append((shift, radix))
        shift += radix.bit_length() - 1
        count //= radix
    return stages


def my_digit(stage):
    return (lax.axis_index("coord") >> stage[0]) & (stage[1] - 1)


def hand_out(table, stage, own, sends):
    digit = my_digit(stage)
    size = own.shape[0]
    own[...] = table[pl.ds(pl.multiple_of(digit * size, 16), size), :]
    for step, send in enumerate(sends, 1):
        begin = pl.multiple_of((digit ^ step) * size, 16)
        send[...] = table[pl.ds(begin, size), :].astype(BF16)


def put_together(own, others, stage, table):
    digit = my_digit(stage)
    size = own.shape[0]
    table[pl.ds(pl.multiple_of(digit * size, 16), size), :] = own[...]
    for step, other in enumerate(others[::-1], 1):
        table[pl.ds(pl.multiple_of((digit ^ step) * size, 16), size), :] = other[...]


def handed_out(rows, rank, stage):
    size = rows // stage[1]
    sends = [jax.ShapeDtypeStruct((size, rank), BF16)] * (stage[1] - 1)
    return [jax.ShapeDtypeStruct((size, rank), F32)] + sends


def fill(table, row):
    if table.shape[0] > row:
        table[row:, :] = jnp.zeros((table.shape[0] - row, table.shape[1]), F32)


def short_kernel(stage, cuts, *refs):
    ins, (x, go), (own, *sends), (a_gate, a_up, b_down, table, sems) = (
        refs[:5], refs[5:7], refs[7:-5], refs[-5:]
    )
    wait = fetch(ins, (x, go, a_gate, a_up, b_down), sems, cuts)
    for which in range(5):
        wait(which)
    tokens = x.shape[0]
    table[:tokens, :] = dot(x[...], a_gate[...], ((1,), (0,)))
    table[tokens : 2 * tokens, :] = dot(x[...], a_up[...], ((1,), (0,)))
    table[2 * tokens : 3 * tokens, :] = dot(go[...], b_down[...], ((1,), (0,)))
    fill(table, 3 * tokens)
    hand_out(table, stage, own, sends)


def short_products(rows, stage, *ins):
    rank = ins[2].shape[1]
    cuts = (2, 2, 1, 1, 1)
    shapes = [jax.ShapeDtypeStruct(a.shape, a.dtype) for a in ins[:2]]
    shapes = shapes + handed_out(rows, rank, stage)
    x, go, *sends = pl.pallas_call(
        functools.partial(short_kernel, stage, cuts),
        out_shape=shapes,
        in_specs=[ANY] * len(ins),
        out_specs=[VMEM] * len(shapes),
        scratch_shapes=[pltpu.VMEM(a.shape, a.dtype) for a in ins[2:]]
        + [pltpu.VMEM((rows, rank), F32), pltpu.SemaphoreType.DMA((sum(cuts),))],
        compiler_params=limit(4),
        cost_estimate=pl.CostEstimate(flops=10**8, bytes_accessed=6 * 10**6, transcendentals=0),
        name="short",
    )(*ins)
    return x, go, sends


def long_kernel(stage, size, *refs):
    ins, held, (own, *sends), (*adapters, table, sems) = refs[:6], refs[6:9], refs[9:-5], refs[-5:]
    rank = table.shape[1]
    spans = [(i, min(i + size, ins[0].shape[0])) for i in range(0, ins[0].shape[0], size)]
    copies = {}

    def begin(slot):
        for part, (first, last) in enumerate(spans):
            pair = []
            for kind, (source, target) in enumerate(
                ((ins[3 + slot], adapters[slot]), (ins[slot], held[slot]))
            ):
                copy = pltpu.make_async_copy(
                    source.at[first:last], target.at[first:last], sems.at[slot, part, kind]
                )
                copy.start()
                pair.append(copy)
            copies[slot, part] = pair

    begin(0)
    begin(1)
    row = 0
    for slot in range(3):
        value = None
        for part, (first, last) in enumerate(spans):
            for copy in copies[slot, part]:
                copy.wait()
            term = dot(adapters[slot][first:last, :].T, held[slot][first:last, :], ((1,), (0,)))
            value = term if value is None else value + term
        if slot == 0:
            begin(2)
        for part in range(value.shape[1] // rank):
            table[row : row + rank, :] = value[:, part * rank : (part + 1) * rank]
            row += rank
    fill(table, row)
    hand_out(table, stage, own, sends)


def long_products(rows, stage, *ins):
    rank = ins[3].shape[1]
    size = min(512, ins[0].shape[0])
    held = [jax.ShapeDtypeStruct(a.shape, a.dtype) for a in ins[:3]]
    shapes = held + handed_out(rows, rank, stage)
    outs = pl.pallas_call(
        functools.partial(long_kernel, stage, size),
        out_shape=shapes,
        in_specs=[ANY] * 6,
        out_specs=[VMEM] * len(shapes),
        scratch_shapes=[pltpu.VMEM(a.shape, a.dtype) for a in ins[3:]]
        + [
            pltpu.VMEM((rows, rank), F32),
            pltpu.SemaphoreType.DMA((3, -(-ins[0].shape[0] // size), 2)),
        ],
        compiler_params=limit(6),
        cost_estimate=pl.CostEstimate(flops=10**9, bytes_accessed=8 * 10**6, transcendentals=0),
        name="long",
    )(*ins)
    return *outs[:3], outs[3:]


def add_kernel(following, count, *refs):
    total = refs[0][...]
    for got in refs[1 : 1 + count]:
        total = total + got[...].astype(F32)
    if following is None:
        refs[1 + count][...] = total.astype(BF16)
    else:
        outs, table = refs[1 + count : -1], refs[-1]
        table[...] = total
        hand_out(table, following, outs[0], outs[1:])


def add_up(own, got, following):
    if following is None:
        shapes, scratch = [jax.ShapeDtypeStruct(own.shape, BF16)], []
    else:
        shapes, scratch = handed_out(*own.shape, following), [pltpu.VMEM(own.shape, F32)]
    return pl.pallas_call(
        functools.partial(add_kernel, following, len(got)),
        out_shape=shapes,
        in_specs=[VMEM] * (1 + len(got)),
        out_specs=[VMEM] * len(shapes),
        scratch_shapes=scratch,
        compiler_params=limit(3),
        name="add_up",
    )(own, *got)


def join_kernel(stage, own, *refs):
    put_together(own, refs[:-1], stage, refs[-1])


def join(own, got, stage):
    return pl.pallas_call(
        functools.partial(join_kernel, stage),
        out_shape=jax.ShapeDtypeStruct((own.shape[0] * stage[1], own.shape[1]), BF16),
        in_specs=[VMEM] * (1 + len(got)),
        out_specs=VMEM,
        compiler_params=limit(3),
        name="join",
    )(own, *got)


def swap(sends, stage):
    return [
        exchange(sends[step - 1], "coord", step << stage[0]) for step in range(stage[1] - 1, 0, -1)
    ]


def after(first, second):
    return lax.optimization_barrier((first, second))[1]


def all_sums(halves, stages, ahead):
    beside = []
    owns = [half[0] for half in halves]
    sends = [half[1:] for half in halves]
    for stage, following in zip(stages, stages[1:] + [None], strict=True):
        got = [swap(send, stage) for send in sends]
        for i in range(len(owns)):
            own = after(owns[0], owns[i]) if i else owns[i]
            owns[i], *sends[i] = add_up(own, got[i], following)
    for stage in stages[:0:-1]:
        got = [swap([own] * (stage[1] - 1), stage) for own in owns]
        for i in range(len(owns)):
            own = after(owns[0], owns[i]) if i else owns[i]
            if stage is stages[1]:
                beside.append(ahead[i](owns[0]))
                own = after(beside[i], own)
            owns[i] = join(own, got[i], stage)
    return beside, [[own] + swap([own] * (stages[0][1] - 1), stages[0]) for own in owns]


def total_over(contrib, count):
    members = lax.axis_size("ckpt")
    contrib = contrib + exchange(contrib, "ckpt", 1)
    apart = 1
    while apart < count:
        flip = apart * members + 1
        pairs = [(source, source ^ flip) for source in range(count * members)]
        contrib = contrib + lax.ppermute(contrib, ("coord", "ckpt"), pairs)
        apart *= 2
    return contrib


def turn_kernel(x, go, x_t, go_t):
    x_t[...] = x[...].T
    go_t[...] = go[...].T


def turn(x, go):
    shape = jax.ShapeDtypeStruct(x.shape[::-1], BF16)
    return pl.pallas_call(
        turn_kernel,
        out_shape=[shape, shape],
        in_specs=[VMEM, VMEM],
        out_specs=[VMEM, VMEM],
        compiler_params=limit(4),
        name="turn",
    )(x, go)


def butterflies(blocks):
    half = 1
    while half < len(blocks):
        done = list(blocks)
        for low in range(len(blocks)):
            if not low & half:
                a, b = blocks[low], blocks[low | half]
                if b is None:
                    done[low], done[low | half] = a, a
                else:
                    done[low], done[low | half] = a + b, a - b
        blocks, half = done, half * 2
    return blocks


def along_block(value, out, row):
    size = value.shape[0]
    tiles = butterflies([value[i : i + 8, :] for i in range(0, size, 8)])
    for i, tile in enumerate(tiles):
        out[row + 8 * i : row + 8 * i + 8, :] = tile
    for begin in range(row, row + size, 64):
        tiles = butterflies([out[pl.ds(begin + j, 8, stride=8), :] for j in range(8)])
        for j, tile in enumerate(tiles):
            out[begin + 8 * j : begin + 8 * j + 8, :] = tile


def signed(value, flags, row):
    return jnp.where(flags[row : row + value.shape[0], :] == 0, value, -value)


def keep(aligned, value, flags, row, out):
    value = signed(value, flags, row)
    if aligned:
        along_block(value, out, row)
    else:
        out[row : row + value.shape[0], :] = value


def wide_kernel(aligned, block, first, stage, *refs):
    parts, refs = refs[: stage[1]], refs[stage[1] :]
    gg, gu, h, flags, out, table = refs
    put_together(parts[0], parts[1:], stage, table)
    tokens = gg.shape[1]
    flags = flags.at[first : first + out.shape[0]]
    row = 0
    for slot, piece in enumerate((gg, gu, h)):
        product = table[slot * tokens : (slot + 1) * tokens, :]
        size = block if aligned else piece.shape[0]
        for begin in range(0, piece.shape[0], size):
            value = dot(piece[begin : begin + size, :], product, ((1,), (0,)))
            keep(aligned, value, flags, row, out)
            row += size


def wide(aligned, block, first, stage, parts, gg, gu, h, flags):
    rank = flags.shape[1]
    return pl.pallas_call(
        functools.partial(wide_kernel, aligned, block, first, stage),
        out_shape=jax.ShapeDtypeStruct((3 * gg.shape[0], rank), F32),
        in_specs=[VMEM] * (len(parts) + 4),
        out_specs=VMEM,
        scratch_shapes=[pltpu.VMEM((parts[0].shape[0] * stage[1], rank), BF16)],
        compiler_params=limit(6),
        cost_estimate=pl.CostEstimate(flops=10**9, bytes_accessed=10**7, transcendentals=0),
        name="wide",
    )(*parts, gg, gu, h, flags)


def rows_kernel(aligned, block, stage, *refs):
    parts, refs = refs[: stage[1]], refs[stage[1] :]
    x_t, go_t, wide_mix, flags, mix, table = refs
    width, tokens = x_t.shape
    first = 3 * width
    length, rank = mix.shape
    put_together(parts[0], parts[1:], stage, table)
    product = [
        jnp.concatenate(
            [table[slot * tokens + part : slot * tokens + part + rank, :] for part in range(0, tokens, rank)],
            axis=1,
        )
        for slot in range(3)
    ]
    size = block if aligned else width
    both = jnp.concatenate(product[:2], axis=0)
    for begin in range(0, width, size):
        value = dot(x_t[begin : begin + size, :], both, ((1,), (1,)))
        keep(aligned, value[:, :rank], flags, begin, mix)
        keep(aligned, value[:, rank:], flags, width + begin, mix)
        value = dot(go_t[begin : begin + size, :], product[2], ((1,), (1,)))
        keep(aligned, value, flags, 2 * width + begin, mix)
    filled = first + wide_mix.shape[0]
    if not aligned:
        mix[first:filled, :] = wide_mix[...]
        mix[filled:, :] = jnp.zeros((length - filled, rank), F32)
        for begin in range(0, length, block):
            along_block(mix[begin : begin + block, :], mix, begin)
    number = length // block
    full = -(-filled // block)

    def load(i, begin):
        if not aligned or i * block < first:
            return mix[pl.ds(i * block + begin, 8), :]
        if i >= full:
            return None
        return wide_mix[pl.ds(i * block - first + begin, 8), :]

    def across(step, _):
        begin = pl.multiple_of(step * 8, 8)
        for i, value in enumerate(butterflies([load(i, begin) for i in range(number)])):
            mix[pl.ds(i * block + begin, 8), :] = value
        return _

    if number > 1:
        lax.fori_loop(0, block // 8, across, 0, unroll=4)


def along_rows(aligned, block, stage, length, parts, x_t, go_t, wide_mix, flags):
    rank = flags.shape[1]
    return pl.pallas_call(
        functools.partial(rows_kernel, aligned, block, stage),
        out_shape=jax.ShapeDtypeStruct((length, rank), F32),
        in_specs=[VMEM] * (len(parts) + 4),
        out_specs=VMEM,
        scratch_shapes=[pltpu.VMEM((parts[0].shape[0] * stage[1], rank), BF16)],
        compiler_params=limit(6),
        name="along_rows",
    )(*parts, x_t, go_t, wide_mix, flags)


def parity(value):
    for fold in (16, 8, 4, 2, 1):
        value = value ^ (value >> fold)
    return value & 1


def signs_kernel(bits, lanes, out):
    rank = out.shape[0]
    device = lax.axis_index("coord") * lax.axis_size("ckpt") + lax.axis_index("ckpt")
    index = lanes[...]

    def sign(bit):
        return (1 - 2 * (bit & 1)).astype(F32)

    low = lax.broadcasted_iota(jnp.int32, (8, index.shape[1]), 0)
    tile = sign(parity((index >> bits) & device))
    for bit in range(3):
        tile = tile * jnp.where((low >> bit & 1) == 0, 1.0, sign(index >> bit))
    tiles = [tile]
    for bit in range(3, rank.bit_length() - 1):
        tiles = tiles + [tile * sign(index >> bit) for tile in tiles]
    out[...] = jnp.concatenate(tiles, axis=0).astype(BF16)


def signs_of(rank, bits, index):
    samples = index.shape[0]
    return pl.pallas_call(
        functools.partial(signs_kernel, bits),
        out_shape=jax.ShapeDtypeStruct((rank, samples), BF16),
        in_specs=[VMEM],
        out_specs=VMEM,
        compiler_params=limit(10),
        name="signs",
    )(index.reshape(1, samples))


def pick_kernel(mix, where, rows):
    samples = rows.shape[0]
    unroll, ahead = min(256, samples), 16

    def pick(step, _):
        begin = step * unroll
        held = []
        for i in range(unroll):
            held.append(mix[where[begin + i]])
            if i >= ahead:
                rows[begin + i - ahead] = held[i - ahead]
        for i in range(unroll - ahead, unroll):
            rows[begin + i] = held[i]
        return _

    lax.fori_loop(0, samples // unroll, pick, 0)


def picked(mix, where):
    rank, samples = mix.shape[1], where.shape[0]
    rows = pl.pallas_call(
        pick_kernel,
        out_shape=jax.ShapeDtypeStruct((samples, 1, rank), F32),
        in_specs=[VMEM, SMEM],
        out_specs=VMEM,
        compiler_params=limit(4),
        name="picked",
    )(mix.reshape(-1, 1, rank), where)
    return rows.reshape(samples, rank)


def sample_kernel(final_scale, rows, signs, out):
    samples, rank = rows.shape
    shape = (rank, rank)
    diagonal = lax.broadcasted_iota(jnp.int32, shape, 0) == lax.broadcasted_iota(jnp.int32, shape, 1)
    for begin in range(0, samples, rank):
        value = rows[begin : begin + rank, :]
        high = value.astype(BF16)
        low = (value - high.astype(F32)).astype(BF16)
        sign = signs[:, begin : begin + rank]
        mixed = dot(
            jnp.concatenate([high, low], axis=1), jnp.concatenate([sign, sign], axis=0), ((1,), (0,))
        )
        chosen = jnp.sum(jnp.where(diagonal, mixed, 0.0), axis=0, keepdims=True)
        out[:, begin : begin + rank] = chosen * final_scale


def sampled(final_scale, rows, signs):
    return pl.pallas_call(
        functools.partial(sample_kernel, final_scale),
        out_shape=jax.ShapeDtypeStruct((1, rows.shape[0]), F32),
        in_specs=[VMEM, VMEM],
        out_specs=VMEM,
        compiler_params=limit(4),
        name="sampled",
    )(rows, signs)


def shards(x, gg, gu, h, go, a_gate, b_gate, a_up, b_up, a_down, b_down, flags, index):
    x, go, gg, gu, h = [a[0, 0] for a in (x, go, gg, gu, h)]
    a_gate, b_gate, a_up, b_up, a_down, b_down = [
        a[0] for a in (a_gate, b_gate, a_up, b_up, a_down, b_down)
    ]
    count = lax.axis_size("coord")
    tokens, rank = x.shape[0], a_gate.shape[1]
    total = flags.shape[0] * count * lax.axis_size("ckpt")
    flags = flags.reshape(-1, rank)
    length = flags.shape[0]
    first = 3 * x.shape[1]
    block = min(256, length)
    aligned = x.shape[1] % block == 0 and gg.shape[0] % block == 0
    where = (index >> (rank.bit_length() - 1)) & (length - 1)
    where = (where & ~63) | (where & 7) << 3 | where >> 3 & 7
    stages = stages_of(count)
    rows = 16 * count * -(-3 * tokens // (16 * count))
    x, go, short = short_products(
        rows, stages[0], *[in_hbm(a) for a in (x, go, a_gate, a_up, b_down)]
    )
    gg, gu, h, long = long_products(
        rows, stages[0], *[in_hbm(a) for a in (gg, gu, h, b_gate, b_up, a_down)]
    )
    flags = after(long[0], flags)
    bits = (length * rank).bit_length() - 1
    ahead = (
        lambda ready: turn(x, go),
        lambda ready: signs_of(rank, bits, after(ready, index)),
    )
    ((x_t, go_t), signs), (short, long) = all_sums([short, long], stages, ahead)
    wide_mix = wide(aligned, block, first, stages[0], short, gg, gu, h, flags)
    final_scale = adapter_scale * float(total) ** -0.5
    mix = along_rows(aligned, block, stages[0], length, long, x_t, go_t, wide_mix, flags)
    contrib = sampled(final_scale, picked(mix, where), signs)
    return total_over(contrib, count)


def solution(mesh):
    in_specs = (
        P("ckpt", "groups", None, "coord"),
        P("ckpt", "groups", "coord", None),
        P("ckpt", "groups", "coord", None),
        P("ckpt", "groups", "coord", None),
        P("ckpt", "groups", None, "coord"),
        P("ckpt", "coord", None),
        P("ckpt", "coord", None),
        P("ckpt", "coord", None),
        P("ckpt", "coord", None),
        P("ckpt", "coord", None),
        P("ckpt", "coord", None),
        P(("coord", "ckpt")),
        P(),
    )
    out_specs = P("groups", None)
    return jax.shard_map(shards, mesh=mesh, in_specs=in_specs, out_specs=out_specs, check_vma=False)
```

profile of v0, /device:TPU:0, one launch (start us, length us, event | category | flops | bytes accessed | tf_op | source)
XLA Modules:
  0.0 60.3 jit_solution(6427715716476528207)
XLA Ops:
  0.0 1.9 %short.1 = (bf16[384,512]{1,0:T(8,128)(2,1)S(1)}, bf16[384,512]{1,0:T(8,128)(2,1)S(1)}, f32[576,128]{1,0:T(8,128)S(1)}, bf16[576,128]{1,0:T(8,128)(2,1)S(1)}) custom-call(bf16[384,512]{1,0:T(8,128)(2,1)} %bitcast.26, bf16[384,512]{1,0:T(8,128)(2,1)} %bitcast.27, bf16[512,128]{1,0:T(8,128)(2,1)} %bitcast.28, bf16[512,128]{1,0:T(8,128)(2,1)} %bitcast.29, ...), custom_call_target="tpu_custom_call" | custom-call | flops 100000000 | bytes 6000000 | tf_op jit(solution)/shard_map/short/pallas_call | solution.py:123
  1.9 3.1 %collective-permute-start = (bf16[576,128]{1,0:T(8,128)(2,1)S(1)}, bf16[576,128]{1,0:T(8,128)(2,1)S(1)}, u32[]{:S(2)}, u32[]{:S(2)}) collective-permute-start(bf16[576,128]{1,0:T(8,128)(2,1)S(1)} %get-tuple-element.36), channel_id=1, source_target_pairs={{0,2},{2,0},{4,6},{6,4},{8,10},{10,8},{12,14},{14,12},{1,3},{3,1},... | collective-permute-start | bytes 442376 | tf_op jit(solution)/shard_map/ppermute | solution.py:30
  5.0 4.1 %long.1 = (bf16[1792,384]{1,0:T(8,128)(2,1)S(1)}, bf16[1792,384]{1,0:T(8,128)(2,1)S(1)}, bf16[1792,384]{1,0:T(8,128)(2,1)S(1)}, f32[576,128]{1,0:T(8,128)S(1)}, bf16[576,128]{1,0:T(8,128)(2,1)S(1)}) custom-call(bf16[1792,384]{1,0:T(8,128)(2,1)} %bitcast.20, bf16[1792,384]{1,0:T(8,128)(2,1)} %bitcast.21, bf16[1792,384]{1,0:T(8,128)(2,1)} %bitcast.22, ...), custom_call_target="tpu_custom_call" | custom-call | flops 1000000000 | bytes 8000000 | tf_op jit(solution)/shard_map/long/pallas_call | solution.py:180
  9.1 0.0 copy-start.1
  9.1 0.1 collective-permute-start.7
  9.2 0.0 collective-permute-done.refs_1_
  9.3 4.1 %collective-permute-start.1 = (bf16[144,128]{1,0:T(8,128)(2,1)S(1)}, bf16[144,128]{1,0:T(8,128)(2,1)S(1)}, u32[]{:S(2)}, u32[]{:S(2)}) collective-permute-start(bf16[144,128]{1,0:T(8,128)(2,1)S(1)} %get-tuple-element.38), channel_id=1, source_target_pairs={{0,12},{2,14},{4,8},{6,10},{8,4},{10,6},{12,0},{14,2},{1,13},{3,15... | collective-permute-start | bytes 110600 | tf_op jit(solution)/shard_map/ppermute | solution.py:30
  13.4 0.0 collective-permute-start.2
  13.4 0.6 %collective-permute-start.3 = (bf16[144,128]{1,0:T(8,128)(2,1)S(1)}, bf16[144,128]{1,0:T(8,128)(2,1)S(1)}, u32[]{:S(2)}, u32[]{:S(2)}) collective-permute-start(bf16[144,128]{1,0:T(8,128)(2,1)S(1)} %get-tuple-element.40), channel_id=1, source_target_pairs={{0,4},{2,6},{4,0},{6,2},{8,12},{10,14},{12,8},{14,10},{1,5},{3,7},... | collective-permute-start | bytes 110600 | tf_op jit(solution)/shard_map/ppermute | solution.py:30
  14.1 0.4 collective-permute-done.7.refs_1_
  14.5 0.0 copy-start
  14.6 1.6 %collective-permute-start.10 = (bf16[144,128]{1,0:T(8,128)(2,1)S(1)}, bf16[144,128]{1,0:T(8,128)(2,1)S(1)}, u32[]{:S(2)}, u32[]{:S(2)}) collective-permute-start(bf16[144,128]{1,0:T(8,128)(2,1)S(1)} %get-tuple-element.50), channel_id=1, source_target_pairs={{0,4},{2,6},{4,0},{6,2},{8,12},{10,14},{12,8},{14,10},{1,5},{3,7},... | collective-permute-start | bytes 110600 | tf_op jit(solution)/shard_map/ppermute | solution.py:30
  16.2 2.5 %collective-permute-start.8 = (bf16[144,128]{1,0:T(8,128)(2,1)S(1)}, bf16[144,128]{1,0:T(8,128)(2,1)S(1)}, u32[]{:S(2)}, u32[]{:S(2)}) collective-permute-start(bf16[144,128]{1,0:T(8,128)(2,1)S(1)} %get-tuple-element.48), channel_id=1, source_target_pairs={{0,12},{2,14},{4,8},{6,10},{8,4},{10,6},{12,0},{14,2},{1,13},{3,15... | collective-permute-start | bytes 110600 | tf_op jit(solution)/shard_map/ppermute | solution.py:30
  18.7 0.0 collective-permute-done.1.refs_1_
  18.7 0.1 collective-permute-start.9
  18.8 0.0 collective-permute-done.2.refs_2_
  18.8 0.0 collective-permute-done.3.refs_3_
  18.8 3.0 %collective-permute-start.4 = (bf16[144,128]{1,0:T(8,128)(2,1)S(1)}, bf16[144,128]{1,0:T(8,128)(2,1)S(1)}, u32[]{:S(2)}, u32[]{:S(2)}) collective-permute-start(bf16[144,128]{1,0:T(8,128)(2,1)S(1)} %add_up.5.own), channel_id=1, source_target_pairs={{0,12},{2,14},{4,8},{6,10},{8,4},{10,6},{12,0},{14,2},{1,13},{3,15... | collective-permute-start | bytes 110600 | tf_op jit(solution)/shard_map/ppermute | solution.py:30
  21.8 0.3 collective-permute-start.5
  22.1 0.0 collective-permute-done.10.refs_3_
  22.2 1.1 %collective-permute-start.6 = (bf16[144,128]{1,0:T(8,128)(2,1)S(1)}, bf16[144,128]{1,0:T(8,128)(2,1)S(1)}, u32[]{:S(2)}, u32[]{:S(2)}) collective-permute-start(bf16[144,128]{1,0:T(8,128)(2,1)S(1)} %add_up.5.own), channel_id=1, source_target_pairs={{0,4},{2,6},{4,0},{6,2},{8,12},{10,14},{12,8},{14,10},{1,5},{3,7},... | collective-permute-start | bytes 110600 | tf_op jit(solution)/shard_map/ppermute | solution.py:30
  23.3 0.0 collective-permute-done.8.refs_1_
  23.3 1.1 %collective-permute-done.9.refs_2_ = bf16[144,128]{1,0:T(8,128)(2,1)S(1)} collective-permute-done((bf16[144,128]{1,0:T(8,128)(2,1)S(1)}, bf16[144,128]{1,0:T(8,128)(2,1)S(1)}, u32[]{:S(2)}, u32[]{:S(2)}) %collective-permute-start.9) | collective-permute-done | bytes 36896 | tf_op jit(solution)/shard_map/ppermute | solution.py:30
  24.4 2.1 %collective-permute-start.11 = (bf16[144,128]{1,0:T(8,128)(2,1)S(1)}, bf16[144,128]{1,0:T(8,128)(2,1)S(1)}, u32[]{:S(2)}, u32[]{:S(2)}) collective-permute-start(bf16[144,128]{1,0:T(8,128)(2,1)S(1)} %add_up.7.own), channel_id=1, source_target_pairs={{0,12},{2,14},{4,8},{6,10},{8,4},{10,6},{12,0},{14,2},{1,13},{3,15... | collective-permute-start | bytes 110600 | tf_op jit(solution)/shard_map/ppermute | solution.py:30
  26.5 0.0 collective-permute-start.12
  26.5 0.0 collective-permute-done.4.refs_0_
  26.5 2.4 %collective-permute-start.13 = (bf16[144,128]{1,0:T(8,128)(2,1)S(1)}, bf16[144,128]{1,0:T(8,128)(2,1)S(1)}, u32[]{:S(2)}, u32[]{:S(2)}) collective-permute-start(bf16[144,128]{1,0:T(8,128)(2,1)S(1)} %add_up.7.own), channel_id=1, source_target_pairs={{0,4},{2,6},{4,0},{6,2},{8,12},{10,14},{12,8},{14,10},{1,5},{3,7},... | collective-permute-start | bytes 110600 | tf_op jit(solution)/shard_map/ppermute | solution.py:30
  28.9 0.3 turn.1
  29.1 0.0 collective-permute-done.5.refs_1_
  29.2 0.0 collective-permute-done.6.refs_2_
  29.2 0.9 %collective-permute-start.15 = (bf16[576,128]{1,0:T(8,128)(2,1)S(1)}, bf16[576,128]{1,0:T(8,128)(2,1)S(1)}, u32[]{:S(2)}, u32[]{:S(2)}) collective-permute-start(bf16[576,128]{1,0:T(8,128)(2,1)S(1)} %join.2.refs_0_), channel_id=1, source_target_pairs={{0,2},{2,0},{4,6},{6,4},{8,10},{10,8},{12,14},{14,12},{1,3},{3,1},... | collective-permute-start | bytes 442376 | tf_op jit(solution)/shard_map/ppermute | solution.py:30
  30.1 0.0 copy-done.1
  30.1 0.5 signs.1
  30.6 0.0 collective-permute-done.11.refs_0_
  30.6 0.8 %collective-permute-done.12.refs_1_ = bf16[144,128]{1,0:T(8,128)(2,1)S(1)} collective-permute-done((bf16[144,128]{1,0:T(8,128)(2,1)S(1)}, bf16[144,128]{1,0:T(8,128)(2,1)S(1)}, u32[]{:S(2)}, u32[]{:S(2)}) %collective-permute-start.12) | collective-permute-done | bytes 36896 | tf_op jit(solution)/shard_map/ppermute | solution.py:30
  31.4 0.0 collective-permute-done.13.refs_2_
  31.4 1.1 %collective-permute-start.14 = (bf16[576,128]{1,0:T(8,128)(2,1)S(1)}, bf16[576,128]{1,0:T(8,128)(2,1)S(1)}, u32[]{:S(2)}, u32[]{:S(2)}) collective-permute-start(bf16[576,128]{1,0:T(8,128)(2,1)S(1)} %join.3.refs_0_), channel_id=1, source_target_pairs={{0,2},{2,0},{4,6},{6,4},{8,10},{10,8},{12,14},{14,12},{1,3},{3,1},... | collective-permute-start | bytes 442376 | tf_op jit(solution)/shard_map/ppermute | solution.py:30
  32.5 1.9 %collective-permute-done.15.refs_1_ = bf16[576,128]{1,0:T(8,128)(2,1)S(1)} collective-permute-done((bf16[576,128]{1,0:T(8,128)(2,1)S(1)}, bf16[576,128]{1,0:T(8,128)(2,1)S(1)}, u32[]{:S(2)}, u32[]{:S(2)}) %collective-permute-start.15) | collective-permute-done | bytes 147488 | tf_op jit(solution)/shard_map/ppermute | solution.py:30
  34.4 0.0 copy-done
  34.4 2.0 %wide.1.refs_4_ = f32[5376,128]{1,0:T(8,128)S(1)} custom-call(bf16[576,128]{1,0:T(8,128)(2,1)S(1)} %join.2.refs_0_, bf16[576,128]{1,0:T(8,128)(2,1)S(1)} %collective-permute-done.15.refs_1_, bf16[1792,384]{1,0:T(8,128)(2,1)S(1)} %get-tuple-element.53.refs_2_, bf16[1792,384]{1,0:T(8,128)(2,1)S(1)} %get-tuple-element.54.refs_3_, ...), custom_call_target="tpu_custom_call" | custom-call | flops 1000000000 | bytes 10000000 | tf_op jit(solution)/shard_map/wide/pallas_call | solution.py:355
  36.4 0.2 collective-permute-done.14.refs_1_
  36.6 1.5 %along_rows.1 = f32[8192,128]{1,0:T(8,128)S(1)} custom-call(bf16[576,128]{1,0:T(8,128)(2,1)S(1)} %join.3.refs_0_, bf16[576,128]{1,0:T(8,128)(2,1)S(1)} %collective-permute-done.14.refs_1_, bf16[512,384]{1,0:T(8,128)(2,1)S(1)} %get-tuple-element.33.refs_2_, bf16[512,384]{1,0:T(8,128)(2,1)S(1)} %get-tuple-element.34.refs_3_, f32[5376,128]{1,0:T(8,128)S(1)} %wide.1.refs_4_, ...), custom_call_target="tpu_custom_call" | custom-call | tf_op jit(solution)/shard_map/along_rows/pallas_call | solution.py:417
  38.2 7.7 %picked.1 = f32[8192,1,128]{2,1,0:T(1,128)S(1)} custom-call(f32[8192,1,128]{2,1,0:T(1,128)S(1)} %bitcast.15, s32[8192]{0:T(1024)S(1)} %and_or_fusion.where), custom_call_target="tpu_custom_call" | custom-call | tf_op jit(solution)/shard_map/picked/pallas_call | solution.py:484
  45.8 1.3 %sampled.1 = f32[1,8192]{1,0:T(1,128)S(1)} custom-call(f32[8192,128]{1,0:T(8,128)S(1)} %bitcast.18, bf16[128,8192]{1,0:T(8,128)(2,1)S(1)} %signs.1), custom_call_target="tpu_custom_call" | custom-call | tf_op jit(solution)/shard_map/sampled/pallas_call | solution.py:512
  47.1 0.1 collective-permute-start.16
  47.2 1.2 %collective-permute-done.16 = f32[1,8192]{1,0:T(1,128)S(1)} collective-permute-done((f32[1,8192]{1,0:T(1,128)S(1)}, f32[1,8192]{1,0:T(1,128)S(1)}, u32[]{:S(2)}, u32[]{:S(2)}) %collective-permute-start.16) | collective-permute-done | bytes 32800 | tf_op jit(solution)/shard_map/ppermute | solution.py:30
  48.4 0.9 %collective-permute-start.17 = (f32[1,8192]{1,0:T(1,128)S(1)}, f32[1,8192]{1,0:T(1,128)S(1)}, u32[]{:S(2)}, u32[]{:S(2)}) collective-permute-start(f32[1,8192]{1,0:T(1,128)S(1)} %add.12), channel_id=1, source_target_pairs={{0,3},{1,2},{2,1},{3,0},{4,7},{5,6},{6,5},{7,4},{8,11},{9,10},{10,... | collective-permute-start | bytes 98312 | tf_op jit(solution)/shard_map/ppermute | solution.py:277
  49.3 2.5 %collective-permute-done.17 = f32[1,8192]{1,0:T(1,128)S(1)} collective-permute-done((f32[1,8192]{1,0:T(1,128)S(1)}, f32[1,8192]{1,0:T(1,128)S(1)}, u32[]{:S(2)}, u32[]{:S(2)}) %collective-permute-start.17) | collective-permute-done | bytes 32800 | tf_op jit(solution)/shard_map/ppermute | solution.py:277
  51.9 1.3 %collective-permute-start.18 = (f32[1,8192]{1,0:T(1,128)S(1)}, f32[1,8192]{1,0:T(1,128)S(1)}, u32[]{:S(2)}, u32[]{:S(2)}) collective-permute-start(f32[1,8192]{1,0:T(1,128)S(1)} %add.13), channel_id=1, source_target_pairs={{0,5},{1,4},{2,7},{3,6},{4,1},{5,0},{6,3},{7,2},{8,13},{9,12},{10,... | collective-permute-start | bytes 98312 | tf_op jit(solution)/shard_map/ppermute | solution.py:277
  53.2 2.1 %collective-permute-done.18 = f32[1,8192]{1,0:T(1,128)S(1)} collective-permute-done((f32[1,8192]{1,0:T(1,128)S(1)}, f32[1,8192]{1,0:T(1,128)S(1)}, u32[]{:S(2)}, u32[]{:S(2)}) %collective-permute-start.18) | collective-permute-done | bytes 32800 | tf_op jit(solution)/shard_map/ppermute | solution.py:277
  55.3 1.9 %collective-permute-start.19 = (f32[1,8192]{1,0:T(1,128)S(1)}, f32[1,8192]{1,0:T(1,128)S(1)}, u32[]{:S(2)}, u32[]{:S(2)}) collective-permute-start(f32[1,8192]{1,0:T(1,128)S(1)} %add.14), channel_id=1, source_target_pairs={{0,9},{1,8},{2,11},{3,10},{4,13},{5,12},{6,15},{7,14},{8,1},{9,0},... | collective-permute-start | bytes 98312 | tf_op jit(solution)/shard_map/ppermute | solution.py:277
  57.2 2.4 %collective-permute-done.19 = f32[1,8192]{1,0:T(1,128)S(1)} collective-permute-done((f32[1,8192]{1,0:T(1,128)S(1)}, f32[1,8192]{1,0:T(1,128)S(1)}, u32[]{:S(2)}, u32[]{:S(2)}) %collective-permute-start.19) | collective-permute-done | bytes 32800 | tf_op jit(solution)/shard_map/ppermute | solution.py:277
  59.6 0.6 %add.15 = f32[1,8192]{1,0:T(1,128)} add(f32[1,8192]{1,0:T(1,128)S(1)} %add.14, f32[1,8192]{1,0:T(1,128)S(1)} %collective-permute-done.19) | non-fusion elementwise | flops 8192 | bytes 98304 | tf_op jit(solution)/shard_map/add | solution.py:277
  (10 shorter events, 0.3 us)
Async XLA Ops:
  1.9 7.3 %collective-permute-start = (bf16[576,128]{1,0:T(8,128)(2,1)S(1)}, bf16[576,128]{1,0:T(8,128)(2,1)S(1)}, u32[]{:S(2)}, u32[]{:S(2)}) collective-permute-start(bf16[576,128]{1,0:T(8,128)(2,1)S(1)} %get-tuple-element.36), channel_id=1, source_target_pairs={{0,2},{2,0},{4,6},{6,4},{8,10},{10,8},{12,14},{14,12},{1,3},{3,1},... | collective-permute-start | bytes 442376 | tf_op jit(solution)/shard_map/ppermute | solution.py:30
  9.1 21.0 %copy-start.1 = (s32[8192]{0:T(1024)S(1)}, s32[8192]{0:T(1024)}, u32[]{:S(2)}) copy-start(s32[8192]{0:T(1024)} %param.25) | copy-start | bytes 98308
  9.1 5.4 %collective-permute-start.7 = (bf16[576,128]{1,0:T(8,128)(2,1)S(1)}, bf16[576,128]{1,0:T(8,128)(2,1)S(1)}, u32[]{:S(2)}, u32[]{:S(2)}) collective-permute-start(bf16[576,128]{1,0:T(8,128)(2,1)S(1)} %get-tuple-element.45), channel_id=1, source_target_pairs={{0,2},{2,0},{4,6},{6,4},{8,10},{10,8},{12,14},{14,12},{1,3},{3,1},... | collective-permute-start | bytes 442376 | tf_op jit(solution)/shard_map/ppermute | solution.py:30
  9.3 9.4 %collective-permute-start.1 = (bf16[144,128]{1,0:T(8,128)(2,1)S(1)}, bf16[144,128]{1,0:T(8,128)(2,1)S(1)}, u32[]{:S(2)}, u32[]{:S(2)}) collective-permute-start(bf16[144,128]{1,0:T(8,128)(2,1)S(1)} %get-tuple-element.38), channel_id=1, source_target_pairs={{0,12},{2,14},{4,8},{6,10},{8,4},{10,6},{12,0},{14,2},{1,13},{3,15... | collective-permute-start | bytes 110600 | tf_op jit(solution)/shard_map/ppermute | solution.py:30
  13.4 5.4 %collective-permute-start.2 = (bf16[144,128]{1,0:T(8,128)(2,1)S(1)}, bf16[144,128]{1,0:T(8,128)(2,1)S(1)}, u32[]{:S(2)}, u32[]{:S(2)}) collective-permute-start(bf16[144,128]{1,0:T(8,128)(2,1)S(1)} %get-tuple-element.39), channel_id=1, source_target_pairs={{0,8},{2,10},{4,12},{6,14},{8,0},{10,2},{12,4},{14,6},{1,9},{3,11}... | collective-permute-start | bytes 110600 | tf_op jit(solution)/shard_map/ppermute | solution.py:30
  13.4 5.4 %collective-permute-start.3 = (bf16[144,128]{1,0:T(8,128)(2,1)S(1)}, bf16[144,128]{1,0:T(8,128)(2,1)S(1)}, u32[]{:S(2)}, u32[]{:S(2)}) collective-permute-start(bf16[144,128]{1,0:T(8,128)(2,1)S(1)} %get-tuple-element.40), channel_id=1, source_target_pairs={{0,4},{2,6},{4,0},{6,2},{8,12},{10,14},{12,8},{14,10},{1,5},{3,7},... | collective-permute-start | bytes 110600 | tf_op jit(solution)/shard_map/ppermute | solution.py:30
  14.5 19.9 %copy-start = (s32[1048576]{0:T(1024)S(1)}, s32[1048576]{0:T(1024)}, u32[]{:S(2)}) copy-start(s32[1048576]{0:T(1024)} %param.24) | copy-start | bytes 12582916
  14.6 7.6 %collective-permute-start.10 = (bf16[144,128]{1,0:T(8,128)(2,1)S(1)}, bf16[144,128]{1,0:T(8,128)(2,1)S(1)}, u32[]{:S(2)}, u32[]{:S(2)}) collective-permute-start(bf16[144,128]{1,0:T(8,128)(2,1)S(1)} %get-tuple-element.50), channel_id=1, source_target_pairs={{0,4},{2,6},{4,0},{6,2},{8,12},{10,14},{12,8},{14,10},{1,5},{3,7},... | collective-permute-start | bytes 110600 | tf_op jit(solution)/shard_map/ppermute | solution.py:30
  16.2 7.1 %collective-permute-start.8 = (bf16[144,128]{1,0:T(8,128)(2,1)S(1)}, bf16[144,128]{1,0:T(8,128)(2,1)S(1)}, u32[]{:S(2)}, u32[]{:S(2)}) collective-permute-start(bf16[144,128]{1,0:T(8,128)(2,1)S(1)} %get-tuple-element.48), channel_id=1, source_target_pairs={{0,12},{2,14},{4,8},{6,10},{8,4},{10,6},{12,0},{14,2},{1,13},{3,15... | collective-permute-start | bytes 110600 | tf_op jit(solution)/shard_map/ppermute | solution.py:30
  18.7 5.7 %collective-permute-start.9 = (bf16[144,128]{1,0:T(8,128)(2,1)S(1)}, bf16[144,128]{1,0:T(8,128)(2,1)S(1)}, u32[]{:S(2)}, u32[]{:S(2)}) collective-permute-start(bf16[144,128]{1,0:T(8,128)(2,1)S(1)} %get-tuple-element.49), channel_id=1, source_target_pairs={{0,8},{2,10},{4,12},{6,14},{8,0},{10,2},{12,4},{14,6},{1,9},{3,11}... | collective-permute-start | bytes 110600 | tf_op jit(solution)/shard_map/ppermute | solution.py:30
  18.8 7.7 %collective-permute-start.4 = (bf16[144,128]{1,0:T(8,128)(2,1)S(1)}, bf16[144,128]{1,0:T(8,128)(2,1)S(1)}, u32[]{:S(2)}, u32[]{:S(2)}) collective-permute-start(bf16[144,128]{1,0:T(8,128)(2,1)S(1)} %add_up.5.own), channel_id=1, source_target_pairs={{0,12},{2,14},{4,8},{6,10},{8,4},{10,6},{12,0},{14,2},{1,13},{3,15... | collective-permute-start | bytes 110600 | tf_op jit(solution)/shard_map/ppermute | solution.py:30
  21.8 7.3 %collective-permute-start.5 = (bf16[144,128]{1,0:T(8,128)(2,1)S(1)}, bf16[144,128]{1,0:T(8,128)(2,1)S(1)}, u32[]{:S(2)}, u32[]{:S(2)}) collective-permute-start(bf16[144,128]{1,0:T(8,128)(2,1)S(1)} %add_up.5.own), channel_id=1, source_target_pairs={{0,8},{2,10},{4,12},{6,14},{8,0},{10,2},{12,4},{14,6},{1,9},{3,11}... | collective-permute-start | bytes 110600 | tf_op jit(solution)/shard_map/ppermute | solution.py:30
  22.2 7.0 %collective-permute-start.6 = (bf16[144,128]{1,0:T(8,128)(2,1)S(1)}, bf16[144,128]{1,0:T(8,128)(2,1)S(1)}, u32[]{:S(2)}, u32[]{:S(2)}) collective-permute-start(bf16[144,128]{1,0:T(8,128)(2,1)S(1)} %add_up.5.own), channel_id=1, source_target_pairs={{0,4},{2,6},{4,0},{6,2},{8,12},{10,14},{12,8},{14,10},{1,5},{3,7},... | collective-permute-start | bytes 110600 | tf_op jit(solution)/shard_map/ppermute | solution.py:30
  24.4 6.2 %collective-permute-start.11 = (bf16[144,128]{1,0:T(8,128)(2,1)S(1)}, bf16[144,128]{1,0:T(8,128)(2,1)S(1)}, u32[]{:S(2)}, u32[]{:S(2)}) collective-permute-start(bf16[144,128]{1,0:T(8,128)(2,1)S(1)} %add_up.7.own), channel_id=1, source_target_pairs={{0,12},{2,14},{4,8},{6,10},{8,4},{10,6},{12,0},{14,2},{1,13},{3,15... | collective-permute-start | bytes 110600 | tf_op jit(solution)/shard_map/ppermute | solution.py:30
  26.5 4.9 %collective-permute-start.12 = (bf16[144,128]{1,0:T(8,128)(2,1)S(1)}, bf16[144,128]{1,0:T(8,128)(2,1)S(1)}, u32[]{:S(2)}, u32[]{:S(2)}) collective-permute-start(bf16[144,128]{1,0:T(8,128)(2,1)S(1)} %add_up.7.own), channel_id=1, source_target_pairs={{0,8},{2,10},{4,12},{6,14},{8,0},{10,2},{12,4},{14,6},{1,9},{3,11}... | collective-permute-start | bytes 110600 | tf_op jit(solution)/shard_map/ppermute | solution.py:30
  26.5 4.9 %collective-permute-start.13 = (bf16[144,128]{1,0:T(8,128)(2,1)S(1)}, bf16[144,128]{1,0:T(8,128)(2,1)S(1)}, u32[]{:S(2)}, u32[]{:S(2)}) collective-permute-start(bf16[144,128]{1,0:T(8,128)(2,1)S(1)} %add_up.7.own), channel_id=1, source_target_pairs={{0,4},{2,6},{4,0},{6,2},{8,12},{10,14},{12,8},{14,10},{1,5},{3,7},... | collective-permute-start | bytes 110600 | tf_op jit(solution)/shard_map/ppermute | solution.py:30
  29.2 5.2 %collective-permute-start.15 = (bf16[576,128]{1,0:T(8,128)(2,1)S(1)}, bf16[576,128]{1,0:T(8,128)(2,1)S(1)}, u32[]{:S(2)}, u32[]{:S(2)}) collective-permute-start(bf16[576,128]{1,0:T(8,128)(2,1)S(1)} %join.2.refs_0_), channel_id=1, source_target_pairs={{0,2},{2,0},{4,6},{6,4},{8,10},{10,8},{12,14},{14,12},{1,3},{3,1},... | collective-permute-start | bytes 442376 | tf_op jit(solution)/shard_map/ppermute | solution.py:30
  31.4 5.2 %collective-permute-start.14 = (bf16[576,128]{1,0:T(8,128)(2,1)S(1)}, bf16[576,128]{1,0:T(8,128)(2,1)S(1)}, u32[]{:S(2)}, u32[]{:S(2)}) collective-permute-start(bf16[576,128]{1,0:T(8,128)(2,1)S(1)} %join.3.refs_0_), channel_id=1, source_target_pairs={{0,2},{2,0},{4,6},{6,4},{8,10},{10,8},{12,14},{14,12},{1,3},{3,1},... | collective-permute-start | bytes 442376 | tf_op jit(solution)/shard_map/ppermute | solution.py:30
  47.1 1.3 %collective-permute-start.16 = (f32[1,8192]{1,0:T(1,128)S(1)}, f32[1,8192]{1,0:T(1,128)S(1)}, u32[]{:S(2)}, u32[]{:S(2)}) collective-permute-start(f32[1,8192]{1,0:T(1,128)S(1)} %sampled.1), channel_id=1, source_target_pairs={{0,1},{1,0},{2,3},{3,2},{4,5},{5,4},{6,7},{7,6},{8,9},{9,8},{10,11... | collective-permute-start | bytes 98312 | tf_op jit(solution)/shard_map/ppermute | solution.py:30
  48.4 3.4 %collective-permute-start.17 = (f32[1,8192]{1,0:T(1,128)S(1)}, f32[1,8192]{1,0:T(1,128)S(1)}, u32[]{:S(2)}, u32[]{:S(2)}) collective-permute-start(f32[1,8192]{1,0:T(1,128)S(1)} %add.12), channel_id=1, source_target_pairs={{0,3},{1,2},{2,1},{3,0},{4,7},{5,6},{6,5},{7,4},{8,11},{9,10},{10,... | collective-permute-start | bytes 98312 | tf_op jit(solution)/shard_map/ppermute | solution.py:277
  51.9 3.4 %collective-permute-start.18 = (f32[1,8192]{1,0:T(1,128)S(1)}, f32[1,8192]{1,0:T(1,128)S(1)}, u32[]{:S(2)}, u32[]{:S(2)}) collective-permute-start(f32[1,8192]{1,0:T(1,128)S(1)} %add.13), channel_id=1, source_target_pairs={{0,5},{1,4},{2,7},{3,6},{4,1},{5,0},{6,3},{7,2},{8,13},{9,12},{10,... | collective-permute-start | bytes 98312 | tf_op jit(solution)/shard_map/ppermute | solution.py:277
  55.3 4.3 %collective-permute-start.19 = (f32[1,8192]{1,0:T(1,128)S(1)}, f32[1,8192]{1,0:T(1,128)S(1)}, u32[]{:S(2)}, u32[]{:S(2)}) collective-permute-start(f32[1,8192]{1,0:T(1,128)S(1)} %add.14), channel_id=1, source_target_pairs={{0,9},{1,8},{2,11},{3,10},{4,13},{5,12},{6,15},{7,14},{8,1},{9,0},... | collective-permute-start | bytes 98312 | tf_op jit(solution)/shard_map/ppermute | solution.py:277
where the time goes:
time: 60.4 us; the launch traced here: 60.3 us
  starting transfers between devices  27.2 us (45%)
  Pallas kernels  19.4 us (32%)
  waiting for transfers between devices  12.7 us (21%)
  other arithmetic  0.77 us (1%)
    ppermute x17, starting transfers between devices, exchange(): return lax.ppermute(value, axis, pairs)  23.1 us
    pallas_call x1, Pallas kernels, picked(): pl.pallas_call(pick_kernel, out_shape=jax.ShapeDtypeStruct((samples, 1, r...  7.68 us
    ppermute x3, waiting for transfers between devices, total_over(): contrib = contrib + lax.ppermute(contrib, ('coord', 'ckpt'), pairs)  7.06 us
    ppermute x17, waiting for transfers between devices, exchange(): return lax.ppermute(value, axis, pairs)  5.65 us
    pallas_call x1, Pallas kernels, long_products(): pl.pallas_call(functools.partial(long_kernel, stage, size), out_shape=sha...  4.13 us
    ppermute x3, starting transfers between devices, total_over(): contrib = contrib + lax.ppermute(contrib, ('coord', 'ckpt'), pairs)  4.06 us
    pallas_call x1, Pallas kernels, wide(): pl.pallas_call(functools.partial(wide_kernel, aligned, block, first, stag...  1.98 us
    pallas_call x1, Pallas kernels, short_products(): pl.pallas_call(functools.partial(short_kernel, stage, cuts), out_shape=sh...  1.9 us
  transfers between devices with their start and end apart: 20, of which 9 were waited for; matrix products, arithmetic and copies ran while one was open for 0% of the time, Pallas kernels for 12%

commit v1 on v0

--- a/solution.py
+++ b/solution.py
@@ -101,70 +101,54 @@
 
 
 def short_kernel(stage, cuts, *refs):
-    ins, (x, go), (own, *sends), (a_gate, a_up, b_down, table, sems) = (
-        refs[:5], refs[5:7], refs[7:-5], refs[-5:]
+    ins, held, (own, *sends), (a_gate, a_up, b_down, table, sems) = (
+        refs[:7], refs[7:11], refs[11:-5], refs[-5:]
     )
-    wait = fetch(ins, (x, go, a_gate, a_up, b_down), sems, cuts)
-    for which in range(5):
+    x, go, gg, b_gate = held
+    wait = fetch(ins, (x, go, a_gate, a_up, b_down, gg, b_gate), sems, cuts)
+    tokens = x.shape[0]
+    for place, (which, left, right) in enumerate(((2, x, a_gate), (3, x, a_up), (4, go, b_down))):
+        if place != 1:
+            wait(place // 2)
         wait(which)
-    tokens = x.shape[0]
-    table[:tokens, :] = dot(x[...], a_gate[...], ((1,), (0,)))
-    table[tokens : 2 * tokens, :] = dot(x[...], a_up[...], ((1,), (0,)))
-    table[2 * tokens : 3 * tokens, :] = dot(go[...], b_down[...], ((1,), (0,)))
+        table[place * tokens : (place + 1) * tokens, :] = dot(left[...], right[...], ((1,), (0,)))
     fill(table, 3 * tokens)
     hand_out(table, stage, own, sends)
+    wait(5)
+    wait(6)
 
 
 def short_products(rows, stage, *ins):
     rank = ins[2].shape[1]
-    cuts = (2, 2, 1, 1, 1)
-    shapes = [jax.ShapeDtypeStruct(a.shape, a.dtype) for a in ins[:2]]
+    cuts = (2, 2, 1, 1, 1, 4, 1)
+    shapes = [jax.ShapeDtypeStruct(ins[i].shape, ins[i].dtype) for i in (0, 1, 5, 6)]
     shapes = shapes + handed_out(rows, rank, stage)
-    x, go, *sends = pl.pallas_call(
+    outs = pl.pallas_call(
         functools.partial(short_kernel, stage, cuts),
         out_shape=shapes,
         in_specs=[ANY] * len(ins),
         out_specs=[VMEM] * len(shapes),
-        scratch_shapes=[pltpu.VMEM(a.shape, a.dtype) for a in ins[2:]]
+        scratch_shapes=[pltpu.VMEM(a.shape, a.dtype) for a in ins[2:5]]
         + [pltpu.VMEM((rows, rank), F32), pltpu.SemaphoreType.DMA((sum(cuts),))],
-        compiler_params=limit(4),
+        compiler_params=limit(5),
         cost_estimate=pl.CostEstimate(flops=10**8, bytes_accessed=6 * 10**6, transcendentals=0),
         name="short",
     )(*ins)
-    return x, go, sends
-
-
-def long_kernel(stage, size, *refs):
-    ins, held, (own, *sends), (*adapters, table, sems) = refs[:6], refs[6:9], refs[9:-5], refs[-5:]
+    return outs[:4], outs[4:]
+
+
+def long_kernel(stage, cuts, gg, b_gate, gu, b_up, h, a_down, *refs):
+    held, (own, *sends), (t_up, t_down, table, sems) = refs[:2], refs[2:-4], refs[-4:]
+    wait = fetch((b_up, gu, a_down, h), (t_up, held[0], t_down, held[1]), sems, cuts)
     rank = table.shape[1]
-    spans = [(i, min(i + size, ins[0].shape[0])) for i in range(0, ins[0].shape[0], size)]
-    copies = {}
-
-    def begin(slot):
-        for part, (first, last) in enumerate(spans):
-            pair = []
-            for kind, (source, target) in enumerate(
-                ((ins[3 + slot], adapters[slot]), (ins[slot], held[slot]))
-            ):
-                copy = pltpu.make_async_copy(
-                    source.at[first:last], target.at[first:last], sems.at[slot, part, kind]
-                )
-                copy.start()
-                pair.append(copy)
-            copies[slot, part] = pair
-
-    begin(0)
-    begin(1)
     row = 0
-    for slot in range(3):
-        value = None
-        for part, (first, last) in enumerate(spans):
-            for copy in copies[slot, part]:
-                copy.wait()
-            term = dot(adapters[slot][first:last, :].T, held[slot][first:last, :], ((1,), (0,)))
-            value = term if value is None else value + term
-        if slot == 0:
-            begin(2)
+    for slot, (wide_ref, adapter) in enumerate(((gg, b_gate), (held[0], t_up), (held[1], t_down))):
+        if slot:
+            wait(2 * slot - 2)
+        turned = adapter[...].T
+        if slot:
+            wait(2 * slot - 1)
+        value = dot(turned, wide_ref[...], ((1,), (0,)))
         for part in range(value.shape[1] // rank):
             table[row : row + rank, :] = value[:, part * rank : (part + 1) * rank]
             row += rank
@@ -172,26 +156,23 @@
     hand_out(table, stage, own, sends)
 
 
-def long_products(rows, stage, *ins):
-    rank = ins[3].shape[1]
-    size = min(512, ins[0].shape[0])
-    held = [jax.ShapeDtypeStruct(a.shape, a.dtype) for a in ins[:3]]
-    shapes = held + handed_out(rows, rank, stage)
+def long_products(rows, stage, gg, b_gate, *ins):
+    rank = b_gate.shape[1]
+    cuts = (1, 4, 1, 4)
+    shapes = [jax.ShapeDtypeStruct(a.shape, a.dtype) for a in (ins[0], ins[2])]
+    shapes = shapes + handed_out(rows, rank, stage)
     outs = pl.pallas_call(
-        functools.partial(long_kernel, stage, size),
+        functools.partial(long_kernel, stage, cuts),
         out_shape=shapes,
-        in_specs=[ANY] * 6,
+        in_specs=[VMEM] * 2 + [ANY] * 4,
         out_specs=[VMEM] * len(shapes),
-        scratch_shapes=[pltpu.VMEM(a.shape, a.dtype) for a in ins[3:]]
-        + [
-            pltpu.VMEM((rows, rank), F32),
-            pltpu.SemaphoreType.DMA((3, -(-ins[0].shape[0] // size), 2)),
-        ],
+        scratch_shapes=[pltpu.VMEM(a.shape, a.dtype) for a in (ins[1], ins[3])]
+        + [pltpu.VMEM((rows, rank), F32), pltpu.SemaphoreType.DMA((sum(cuts),))],
         compiler_params=limit(6),
         cost_estimate=pl.CostEstimate(flops=10**9, bytes_accessed=8 * 10**6, transcendentals=0),
         name="long",
-    )(*ins)
-    return *outs[:3], outs[3:]
+    )(gg, b_gate, *ins)
+    return *outs[:2], outs[2:]
 
 
 def add_kernel(following, count, *refs):
@@ -255,7 +236,8 @@
         got = [swap(send, stage) for send in sends]
         for i in range(len(owns)):
             own = after(owns[0], owns[i]) if i else owns[i]
-            owns[i], *sends[i] = add_up(own, got[i], following)
+            order = got[i][1:] + got[i][:1] if i else got[i]
+            owns[i], *sends[i] = add_up(own, order, following)
     for stage in stages[:0:-1]:
         got = [swap([own] * (stage[1] - 1), stage) for own in owns]
         for i in range(len(owns)):
@@ -466,14 +448,15 @@
     unroll, ahead = min(256, samples), 16
 
     def pick(step, _):
-        begin = step * unroll
+        span = pl.ds(pl.multiple_of(step * unroll, unroll), unroll)
+        sources, targets = where.at[span], rows.at[span]
         held = []
         for i in range(unroll):
-            held.append(mix[where[begin + i]])
+            held.append(mix[sources[i]])
             if i >= ahead:
-                rows[begin + i - ahead] = held[i - ahead]
+                targets[i - ahead] = held[i - ahead]
         for i in range(unroll - ahead, unroll):
-            rows[begin + i] = held[i]
+            targets[i] = held[i]
         return _
 
     lax.fori_loop(0, samples // unroll, pick, 0)
@@ -536,11 +519,11 @@
     where = (where & ~63) | (where & 7) << 3 | where >> 3 & 7
     stages = stages_of(count)
     rows = 16 * count * -(-3 * tokens // (16 * count))
-    x, go, short = short_products(
-        rows, stages[0], *[in_hbm(a) for a in (x, go, a_gate, a_up, b_down)]
+    (x, go, gg, b_gate), short = short_products(
+        rows, stages[0], *[in_hbm(a) for a in (x, go, a_gate, a_up, b_down, gg, b_gate)]
     )
-    gg, gu, h, long = long_products(
-        rows, stages[0], *[in_hbm(a) for a in (gg, gu, h, b_gate, b_up, a_down)]
+    gu, h, long = long_products(
+        rows, stages[0], gg, b_gate, *[in_hbm(a) for a in (gu, b_up, h, a_down)]
     )
     flags = after(long[0], flags)
     bits = (length * rank).bit_length() - 1

time: 60.4 us -> 61.2 us (1.013)
  starting transfers between devices: 27.2 us -> 28 us
  waiting for transfers between devices: 12.7 us -> 13.5 us
  Pallas kernels: 19.4 us -> 18.6 us
    ppermute x17, starting transfers between devices: 23.1 us -> 24.6 us  [exchange(): return lax.ppermute(value, axis, pairs)]
    pallas_call x1, Pallas kernels: 4.13 us -> 2.83 us  [long_products(): pl.pallas_call(functools.partial(long_kernel, stage, cuts), out_shape=sha...]
    ppermute x3, waiting for transfers between devices: 7.06 us -> 8.34 us  [total_over(): contrib = contrib + lax.ppermute(contrib, ('coord', 'ckpt'), pairs)]
    ppermute x3, starting transfers between devices: 4.06 us -> 3.35 us  [total_over(): contrib = contrib + lax.ppermute(contrib, ('coord', 'ckpt'), pairs)]
  transfers between devices with their start and end apart: 20 -> 20, of which waited for: 9 -> 7; matrix products, arithmetic and copies ran while one was open for 0% -> 0% of each run, Pallas kernels for 12% -> 9%
where the time goes in v1:
time: 61.2 us; the launch traced here: 61 us
  starting transfers between devices  28 us (46%)
  Pallas kernels  18.6 us (30%)
  waiting for transfers between devices  13.5 us (22%)
  other arithmetic  0.77 us (1%)
    ppermute x17, starting transfers between devices, exchange(): return lax.ppermute(value, axis, pairs)  24.6 us
    ppermute x3, waiting for transfers between devices, total_over(): contrib = contrib + lax.ppermute(contrib, ('coord', 'ckpt'), pairs)  8.34 us
    pallas_call x1, Pallas kernels, picked(): pl.pallas_call(pick_kernel, out_shape=jax.ShapeDtypeStruct((samples, 1, r...  7.69 us
    ppermute x17, waiting for transfers between devices, exchange(): return lax.ppermute(value, axis, pairs)  5.19 us
    ppermute x3, starting transfers between devices, total_over(): contrib = contrib + lax.ppermute(contrib, ('coord', 'ckpt'), pairs)  3.35 us
    pallas_call x1, Pallas kernels, long_products(): pl.pallas_call(functools.partial(long_kernel, stage, cuts), out_shape=sha...  2.83 us
    pallas_call x1, Pallas kernels, short_products(): pl.pallas_call(functools.partial(short_kernel, stage, cuts), out_shape=sh...  2.38 us
    pallas_call x1, Pallas kernels, wide(): pl.pallas_call(functools.partial(wide_kernel, aligned, block, first, stag...  1.98 us
  transfers between devices with their start and end apart: 20, of which 7 were waited for; matrix products, arithmetic and copies ran while one was open for 0% of the time, Pallas kernels for 9%

profile of v1, /device:TPU:0, one launch (start us, length us, event | category | flops | bytes accessed | tf_op | source)
XLA Modules:
  0.0 61.0 jit_solution(5708562041103263964)
XLA Ops:
  0.0 2.4 %short.1 = (bf16[384,512]{1,0:T(8,128)(2,1)S(1)}, bf16[384,512]{1,0:T(8,128)(2,1)S(1)}, bf16[1792,384]{1,0:T(8,128)(2,1)S(1)}, bf16[1792,128]{1,0:T(8,128)(2,1)S...) custom-call(bf16[384,512]{1,0:T(8,128)(2,1)} %bitcast.26, bf16[384,512]{1,0:T(8,128)(2,1)} %bitcast.27, ...), custom_call_target="tpu_custom_call" | custom-call | flops 100000000 | bytes 6000000 | tf_op jit(solution)/shard_map/short/pallas_call | solution.py:126
  2.4 3.0 %collective-permute-start = (bf16[576,128]{1,0:T(8,128)(2,1)S(1)}, bf16[576,128]{1,0:T(8,128)(2,1)S(1)}, u32[]{:S(2)}, u32[]{:S(2)}) collective-permute-start(bf16[576,128]{1,0:T(8,128)(2,1)S(1)} %get-tuple-element.37), channel_id=1, source_target_pairs={{0,2},{2,0},{4,6},{6,4},{8,10},{10,8},{12,14},{14,12},{1,3},{3,1},... | collective-permute-start | bytes 442376 | tf_op jit(solution)/shard_map/ppermute | solution.py:30
  5.4 2.8 %long.1 = (bf16[1792,384]{1,0:T(8,128)(2,1)S(1)}, bf16[1792,384]{1,0:T(8,128)(2,1)S(1)}, f32[576,128]{1,0:T(8,128)S(1)}, bf16[576,128]{1,0:T(8,128)(2,1)S(1)}) custom-call(bf16[1792,384]{1,0:T(8,128)(2,1)S(1)} %get-tuple-element.44.gg.refs_2_, bf16[1792,128]{1,0:T(8,128)(2,1)S(1)} %get-tuple-element.45.b_gate, bf16[1792,384]{1,0:T(8,128)(2,1)} %bitcast.21, ...), custom_call_target="tpu_custom_call" | custom-call | flops 1000000000 | bytes 8000000 | tf_op jit(solution)/shard_map/long/pallas_call | solution.py:164
  8.3 0.0 copy-start.1
  8.3 0.1 collective-permute-start.7
  8.4 0.9 %collective-permute-done.refs_1_ = bf16[576,128]{1,0:T(8,128)(2,1)S(1)} collective-permute-done((bf16[576,128]{1,0:T(8,128)(2,1)S(1)}, bf16[576,128]{1,0:T(8,128)(2,1)S(1)}, u32[]{:S(2)}, u32[]{:S(2)}) %collective-permute-start) | collective-permute-done | bytes 147488 | tf_op jit(solution)/shard_map/ppermute | solution.py:30
  9.3 3.9 %collective-permute-start.1 = (bf16[144,128]{1,0:T(8,128)(2,1)S(1)}, bf16[144,128]{1,0:T(8,128)(2,1)S(1)}, u32[]{:S(2)}, u32[]{:S(2)}) collective-permute-start(bf16[144,128]{1,0:T(8,128)(2,1)S(1)} %get-tuple-element.39), channel_id=1, source_target_pairs={{0,12},{2,14},{4,8},{6,10},{8,4},{10,6},{12,0},{14,2},{1,13},{3,15... | collective-permute-start | bytes 110600 | tf_op jit(solution)/shard_map/ppermute | solution.py:30
  13.2 0.0 collective-permute-start.2
  13.2 0.6 %collective-permute-start.3 = (bf16[144,128]{1,0:T(8,128)(2,1)S(1)}, bf16[144,128]{1,0:T(8,128)(2,1)S(1)}, u32[]{:S(2)}, u32[]{:S(2)}) collective-permute-start(bf16[144,128]{1,0:T(8,128)(2,1)S(1)} %get-tuple-element.41), channel_id=1, source_target_pairs={{0,4},{2,6},{4,0},{6,2},{8,12},{10,14},{12,8},{14,10},{1,5},{3,7},... | collective-permute-start | bytes 110600 | tf_op jit(solution)/shard_map/ppermute | solution.py:30
  13.8 0.0 collective-permute-done.7.refs_1_
  13.8 0.0 copy-start
  13.9 3.8 %collective-permute-start.10 = (bf16[144,128]{1,0:T(8,128)(2,1)S(1)}, bf16[144,128]{1,0:T(8,128)(2,1)S(1)}, u32[]{:S(2)}, u32[]{:S(2)}) collective-permute-start(bf16[144,128]{1,0:T(8,128)(2,1)S(1)} %get-tuple-element.53), channel_id=1, source_target_pairs={{0,12},{2,14},{4,8},{6,10},{8,4},{10,6},{12,0},{14,2},{1,13},{3,15... | collective-permute-start | bytes 110600 | tf_op jit(solution)/shard_map/ppermute | solution.py:30
  17.7 0.0 collective-permute-start.8
  17.7 0.0 collective-permute-done.1.refs_1_
  17.7 0.6 %collective-permute-start.9 = (bf16[144,128]{1,0:T(8,128)(2,1)S(1)}, bf16[144,128]{1,0:T(8,128)(2,1)S(1)}, u32[]{:S(2)}, u32[]{:S(2)}) collective-permute-start(bf16[144,128]{1,0:T(8,128)(2,1)S(1)} %get-tuple-element.52), channel_id=1, source_target_pairs={{0,4},{2,6},{4,0},{6,2},{8,12},{10,14},{12,8},{14,10},{1,5},{3,7},... | collective-permute-start | bytes 110600 | tf_op jit(solution)/shard_map/ppermute | solution.py:30
  18.4 0.0 collective-permute-done.2.refs_2_
  18.4 0.0 collective-permute-done.3.refs_3_
  18.4 3.8 %collective-permute-start.4 = (bf16[144,128]{1,0:T(8,128)(2,1)S(1)}, bf16[144,128]{1,0:T(8,128)(2,1)S(1)}, u32[]{:S(2)}, u32[]{:S(2)}) collective-permute-start(bf16[144,128]{1,0:T(8,128)(2,1)S(1)} %add_up.5.own), channel_id=1, source_target_pairs={{0,12},{2,14},{4,8},{6,10},{8,4},{10,6},{12,0},{14,2},{1,13},{3,15... | collective-permute-start | bytes 110600 | tf_op jit(solution)/shard_map/ppermute | solution.py:30
  22.2 0.0 collective-permute-start.5
  22.2 0.0 collective-permute-done.10.refs_3_
  22.2 0.6 %collective-permute-start.6 = (bf16[144,128]{1,0:T(8,128)(2,1)S(1)}, bf16[144,128]{1,0:T(8,128)(2,1)S(1)}, u32[]{:S(2)}, u32[]{:S(2)}) collective-permute-start(bf16[144,128]{1,0:T(8,128)(2,1)S(1)} %add_up.5.own), channel_id=1, source_target_pairs={{0,4},{2,6},{4,0},{6,2},{8,12},{10,14},{12,8},{14,10},{1,5},{3,7},... | collective-permute-start | bytes 110600 | tf_op jit(solution)/shard_map/ppermute | solution.py:30
  22.8 0.0 collective-permute-done.8.refs_1_
  22.9 0.0 collective-permute-done.9.refs_2_
  22.9 3.8 %collective-permute-start.11 = (bf16[144,128]{1,0:T(8,128)(2,1)S(1)}, bf16[144,128]{1,0:T(8,128)(2,1)S(1)}, u32[]{:S(2)}, u32[]{:S(2)}) collective-permute-start(bf16[144,128]{1,0:T(8,128)(2,1)S(1)} %add_up.7.own), channel_id=1, source_target_pairs={{0,12},{2,14},{4,8},{6,10},{8,4},{10,6},{12,0},{14,2},{1,13},{3,15... | collective-permute-start | bytes 110600 | tf_op jit(solution)/shard_map/ppermute | solution.py:30
  26.7 0.0 collective-permute-start.12
  26.7 0.0 collective-permute-done.4.refs_0_
  26.7 0.6 %collective-permute-start.13 = (bf16[144,128]{1,0:T(8,128)(2,1)S(1)}, bf16[144,128]{1,0:T(8,128)(2,1)S(1)}, u32[]{:S(2)}, u32[]{:S(2)}) collective-permute-start(bf16[144,128]{1,0:T(8,128)(2,1)S(1)} %add_up.7.own), channel_id=1, source_target_pairs={{0,4},{2,6},{4,0},{6,2},{8,12},{10,14},{12,8},{14,10},{1,5},{3,7},... | collective-permute-start | bytes 110600 | tf_op jit(solution)/shard_map/ppermute | solution.py:30
  27.3 0.3 turn.1
  27.6 0.0 collective-permute-done.5.refs_1_
  27.6 0.0 collective-permute-done.6.refs_2_
  27.7 1.9 %collective-permute-start.15 = (bf16[576,128]{1,0:T(8,128)(2,1)S(1)}, bf16[576,128]{1,0:T(8,128)(2,1)S(1)}, u32[]{:S(2)}, u32[]{:S(2)}) collective-permute-start(bf16[576,128]{1,0:T(8,128)(2,1)S(1)} %join.2.refs_0_), channel_id=1, source_target_pairs={{0,2},{2,0},{4,6},{6,4},{8,10},{10,8},{12,14},{14,12},{1,3},{3,1},... | collective-permute-start | bytes 442376 | tf_op jit(solution)/shard_map/ppermute | solution.py:30
  29.6 0.0 copy-done.1
  29.6 0.5 signs.1
  30.0 0.0 collective-permute-done.11.refs_0_
  30.0 1.5 %collective-permute-done.12.refs_1_ = bf16[144,128]{1,0:T(8,128)(2,1)S(1)} collective-permute-done((bf16[144,128]{1,0:T(8,128)(2,1)S(1)}, bf16[144,128]{1,0:T(8,128)(2,1)S(1)}, u32[]{:S(2)}, u32[]{:S(2)}) %collective-permute-start.12) | collective-permute-done | bytes 36896 | tf_op jit(solution)/shard_map/ppermute | solution.py:30
  31.6 0.0 collective-permute-done.13.refs_2_
  31.6 1.6 %collective-permute-start.14 = (bf16[576,128]{1,0:T(8,128)(2,1)S(1)}, bf16[576,128]{1,0:T(8,128)(2,1)S(1)}, u32[]{:S(2)}, u32[]{:S(2)}) collective-permute-start(bf16[576,128]{1,0:T(8,128)(2,1)S(1)} %join.3.refs_0_), channel_id=1, source_target_pairs={{0,2},{2,0},{4,6},{6,4},{8,10},{10,8},{12,14},{14,12},{1,3},{3,1},... | collective-permute-start | bytes 442376 | tf_op jit(solution)/shard_map/ppermute | solution.py:30
  33.2 0.0 collective-permute-done.15.refs_1_
  33.2 0.0 copy-done
  33.2 2.0 %wide.1.refs_4_ = f32[5376,128]{1,0:T(8,128)S(1)} custom-call(bf16[576,128]{1,0:T(8,128)(2,1)S(1)} %join.2.refs_0_, bf16[576,128]{1,0:T(8,128)(2,1)S(1)} %collective-permute-done.15.refs_1_, bf16[1792,384]{1,0:T(8,128)(2,1)S(1)} %get-tuple-element.44.gg.refs_2_, bf16[1792,384]{1,0:T(8,128)(2,1)S(1)} %get-tuple-element.56.refs_3_, ...), custom_call_target="tpu_custom_call" | custom-call | flops 1000000000 | bytes 10000000 | tf_op jit(solution)/shard_map/wide/pallas_call | solution.py:337
  35.2 1.6 %collective-permute-done.14.refs_1_ = bf16[576,128]{1,0:T(8,128)(2,1)S(1)} collective-permute-done((bf16[576,128]{1,0:T(8,128)(2,1)S(1)}, bf16[576,128]{1,0:T(8,128)(2,1)S(1)}, u32[]{:S(2)}, u32[]{:S(2)}) %collective-permute-start.14) | collective-permute-done | bytes 147488 | tf_op jit(solution)/shard_map/ppermute | solution.py:30
  36.8 1.5 %along_rows.1 = f32[8192,128]{1,0:T(8,128)S(1)} custom-call(bf16[576,128]{1,0:T(8,128)(2,1)S(1)} %join.3.refs_0_, bf16[576,128]{1,0:T(8,128)(2,1)S(1)} %collective-permute-done.14.refs_1_, bf16[512,384]{1,0:T(8,128)(2,1)S(1)} %get-tuple-element.34.refs_2_, bf16[512,384]{1,0:T(8,128)(2,1)S(1)} %get-tuple-element.35.refs_3_, f32[5376,128]{1,0:T(8,128)S(1)} %wide.1.refs_4_, ...), custom_call_target="tpu_custom_call" | custom-call | tf_op jit(solution)/shard_map/along_rows/pallas_call | solution.py:399
  38.3 7.7 %picked.1 = f32[8192,1,128]{2,1,0:T(1,128)S(1)} custom-call(f32[8192,1,128]{2,1,0:T(1,128)S(1)} %bitcast.15, s32[8192]{0:T(1024)S(1)} %and_or_fusion.where), custom_call_target="tpu_custom_call" | custom-call | tf_op jit(solution)/shard_map/picked/pallas_call | solution.py:467
  46.0 1.3 %sampled.1 = f32[1,8192]{1,0:T(1,128)S(1)} custom-call(f32[8192,128]{1,0:T(8,128)S(1)} %bitcast.18, bf16[128,8192]{1,0:T(8,128)(2,1)S(1)} %signs.1), custom_call_target="tpu_custom_call" | custom-call | tf_op jit(solution)/shard_map/sampled/pallas_call | solution.py:495
  47.3 0.1 collective-permute-start.16
  47.4 1.2 %collective-permute-done.16 = f32[1,8192]{1,0:T(1,128)S(1)} collective-permute-done((f32[1,8192]{1,0:T(1,128)S(1)}, f32[1,8192]{1,0:T(1,128)S(1)}, u32[]{:S(2)}, u32[]{:S(2)}) %collective-permute-start.16) | collective-permute-done | bytes 32800 | tf_op jit(solution)/shard_map/ppermute | solution.py:30
  48.6 1.4 %collective-permute-start.17 = (f32[1,8192]{1,0:T(1,128)S(1)}, f32[1,8192]{1,0:T(1,128)S(1)}, u32[]{:S(2)}, u32[]{:S(2)}) collective-permute-start(f32[1,8192]{1,0:T(1,128)S(1)} %add.12), channel_id=1, source_target_pairs={{0,3},{1,2},{2,1},{3,0},{4,7},{5,6},{6,5},{7,4},{8,11},{9,10},{10,... | collective-permute-start | bytes 98312 | tf_op jit(solution)/shard_map/ppermute | solution.py:259
  50.0 2.0 %collective-permute-done.17 = f32[1,8192]{1,0:T(1,128)S(1)} collective-permute-done((f32[1,8192]{1,0:T(1,128)S(1)}, f32[1,8192]{1,0:T(1,128)S(1)}, u32[]{:S(2)}, u32[]{:S(2)}) %collective-permute-start.17) | collective-permute-done | bytes 32800 | tf_op jit(solution)/shard_map/ppermute | solution.py:259
  52.1 0.1 collective-permute-start.18
  52.1 3.3 %collective-permute-done.18 = f32[1,8192]{1,0:T(1,128)S(1)} collective-permute-done((f32[1,8192]{1,0:T(1,128)S(1)}, f32[1,8192]{1,0:T(1,128)S(1)}, u32[]{:S(2)}, u32[]{:S(2)}) %collective-permute-start.18) | collective-permute-done | bytes 32800 | tf_op jit(solution)/shard_map/ppermute | solution.py:259
  55.5 1.9 %collective-permute-start.19 = (f32[1,8192]{1,0:T(1,128)S(1)}, f32[1,8192]{1,0:T(1,128)S(1)}, u32[]{:S(2)}, u32[]{:S(2)}) collective-permute-start(f32[1,8192]{1,0:T(1,128)S(1)} %add.14), channel_id=1, source_target_pairs={{0,9},{1,8},{2,11},{3,10},{4,13},{5,12},{6,15},{7,14},{8,1},{9,0},... | collective-permute-start | bytes 98312 | tf_op jit(solution)/shard_map/ppermute | solution.py:259
  57.4 3.0 %collective-permute-done.19 = f32[1,8192]{1,0:T(1,128)S(1)} collective-permute-done((f32[1,8192]{1,0:T(1,128)S(1)}, f32[1,8192]{1,0:T(1,128)S(1)}, u32[]{:S(2)}, u32[]{:S(2)}) %collective-permute-start.19) | collective-permute-done | bytes 32800 | tf_op jit(solution)/shard_map/ppermute | solution.py:259
  60.4 0.6 %add.15 = f32[1,8192]{1,0:T(1,128)} add(f32[1,8192]{1,0:T(1,128)S(1)} %add.14, f32[1,8192]{1,0:T(1,128)S(1)} %collective-permute-done.19) | non-fusion elementwise | flops 8192 | bytes 98304 | tf_op jit(solution)/shard_map/add | solution.py:259
  (10 shorter events, 0.3 us)
Async XLA Ops:
  2.4 6.9 %collective-permute-start = (bf16[576,128]{1,0:T(8,128)(2,1)S(1)}, bf16[576,128]{1,0:T(8,128)(2,1)S(1)}, u32[]{:S(2)}, u32[]{:S(2)}) collective-permute-start(bf16[576,128]{1,0:T(8,128)(2,1)S(1)} %get-tuple-element.37), channel_id=1, source_target_pairs={{0,2},{2,0},{4,6},{6,4},{8,10},{10,8},{12,14},{14,12},{1,3},{3,1},... | collective-permute-start | bytes 442376 | tf_op jit(solution)/shard_map/ppermute | solution.py:30
  8.3 21.3 %copy-start.1 = (s32[8192]{0:T(1024)S(1)}, s32[8192]{0:T(1024)}, u32[]{:S(2)}) copy-start(s32[8192]{0:T(1024)} %param.25) | copy-start | bytes 98308
  8.3 5.6 %collective-permute-start.7 = (bf16[576,128]{1,0:T(8,128)(2,1)S(1)}, bf16[576,128]{1,0:T(8,128)(2,1)S(1)}, u32[]{:S(2)}, u32[]{:S(2)}) collective-permute-start(bf16[576,128]{1,0:T(8,128)(2,1)S(1)} %get-tuple-element.48), channel_id=1, source_target_pairs={{0,2},{2,0},{4,6},{6,4},{8,10},{10,8},{12,14},{14,12},{1,3},{3,1},... | collective-permute-start | bytes 442376 | tf_op jit(solution)/shard_map/ppermute | solution.py:30
  9.3 8.4 %collective-permute-start.1 = (bf16[144,128]{1,0:T(8,128)(2,1)S(1)}, bf16[144,128]{1,0:T(8,128)(2,1)S(1)}, u32[]{:S(2)}, u32[]{:S(2)}) collective-permute-start(bf16[144,128]{1,0:T(8,128)(2,1)S(1)} %get-tuple-element.39), channel_id=1, source_target_pairs={{0,12},{2,14},{4,8},{6,10},{8,4},{10,6},{12,0},{14,2},{1,13},{3,15... | collective-permute-start | bytes 110600 | tf_op jit(solution)/shard_map/ppermute | solution.py:30
  13.2 5.2 %collective-permute-start.2 = (bf16[144,128]{1,0:T(8,128)(2,1)S(1)}, bf16[144,128]{1,0:T(8,128)(2,1)S(1)}, u32[]{:S(2)}, u32[]{:S(2)}) collective-permute-start(bf16[144,128]{1,0:T(8,128)(2,1)S(1)} %get-tuple-element.40), channel_id=1, source_target_pairs={{0,8},{2,10},{4,12},{6,14},{8,0},{10,2},{12,4},{14,6},{1,9},{3,11}... | collective-permute-start | bytes 110600 | tf_op jit(solution)/shard_map/ppermute | solution.py:30
  13.2 5.2 %collective-permute-start.3 = (bf16[144,128]{1,0:T(8,128)(2,1)S(1)}, bf16[144,128]{1,0:T(8,128)(2,1)S(1)}, u32[]{:S(2)}, u32[]{:S(2)}) collective-permute-start(bf16[144,128]{1,0:T(8,128)(2,1)S(1)} %get-tuple-element.41), channel_id=1, source_target_pairs={{0,4},{2,6},{4,0},{6,2},{8,12},{10,14},{12,8},{14,10},{1,5},{3,7},... | collective-permute-start | bytes 110600 | tf_op jit(solution)/shard_map/ppermute | solution.py:30
  13.8 19.4 %copy-start = (s32[1048576]{0:T(1024)S(1)}, s32[1048576]{0:T(1024)}, u32[]{:S(2)}) copy-start(s32[1048576]{0:T(1024)} %param.24) | copy-start | bytes 12582916
  13.9 8.3 %collective-permute-start.10 = (bf16[144,128]{1,0:T(8,128)(2,1)S(1)}, bf16[144,128]{1,0:T(8,128)(2,1)S(1)}, u32[]{:S(2)}, u32[]{:S(2)}) collective-permute-start(bf16[144,128]{1,0:T(8,128)(2,1)S(1)} %get-tuple-element.53), channel_id=1, source_target_pairs={{0,12},{2,14},{4,8},{6,10},{8,4},{10,6},{12,0},{14,2},{1,13},{3,15... | collective-permute-start | bytes 110600 | tf_op jit(solution)/shard_map/ppermute | solution.py:30
  17.7 5.1 %collective-permute-start.8 = (bf16[144,128]{1,0:T(8,128)(2,1)S(1)}, bf16[144,128]{1,0:T(8,128)(2,1)S(1)}, u32[]{:S(2)}, u32[]{:S(2)}) collective-permute-start(bf16[144,128]{1,0:T(8,128)(2,1)S(1)} %get-tuple-element.51), channel_id=1, source_target_pairs={{0,8},{2,10},{4,12},{6,14},{8,0},{10,2},{12,4},{14,6},{1,9},{3,11}... | collective-permute-start | bytes 110600 | tf_op jit(solution)/shard_map/ppermute | solution.py:30
  17.7 5.1 %collective-permute-start.9 = (bf16[144,128]{1,0:T(8,128)(2,1)S(1)}, bf16[144,128]{1,0:T(8,128)(2,1)S(1)}, u32[]{:S(2)}, u32[]{:S(2)}) collective-permute-start(bf16[144,128]{1,0:T(8,128)(2,1)S(1)} %get-tuple-element.52), channel_id=1, source_target_pairs={{0,4},{2,6},{4,0},{6,2},{8,12},{10,14},{12,8},{14,10},{1,5},{3,7},... | collective-permute-start | bytes 110600 | tf_op jit(solution)/shard_map/ppermute | solution.py:30
  18.4 8.3 %collective-permute-start.4 = (bf16[144,128]{1,0:T(8,128)(2,1)S(1)}, bf16[144,128]{1,0:T(8,128)(2,1)S(1)}, u32[]{:S(2)}, u32[]{:S(2)}) collective-permute-start(bf16[144,128]{1,0:T(8,128)(2,1)S(1)} %add_up.5.own), channel_id=1, source_target_pairs={{0,12},{2,14},{4,8},{6,10},{8,4},{10,6},{12,0},{14,2},{1,13},{3,15... | collective-permute-start | bytes 110600 | tf_op jit(solution)/shard_map/ppermute | solution.py:30
  22.2 5.4 %collective-permute-start.5 = (bf16[144,128]{1,0:T(8,128)(2,1)S(1)}, bf16[144,128]{1,0:T(8,128)(2,1)S(1)}, u32[]{:S(2)}, u32[]{:S(2)}) collective-permute-start(bf16[144,128]{1,0:T(8,128)(2,1)S(1)} %add_up.5.own), channel_id=1, source_target_pairs={{0,8},{2,10},{4,12},{6,14},{8,0},{10,2},{12,4},{14,6},{1,9},{3,11}... | collective-permute-start | bytes 110600 | tf_op jit(solution)/shard_map/ppermute | solution.py:30
  22.2 5.4 %collective-permute-start.6 = (bf16[144,128]{1,0:T(8,128)(2,1)S(1)}, bf16[144,128]{1,0:T(8,128)(2,1)S(1)}, u32[]{:S(2)}, u32[]{:S(2)}) collective-permute-start(bf16[144,128]{1,0:T(8,128)(2,1)S(1)} %add_up.5.own), channel_id=1, source_target_pairs={{0,4},{2,6},{4,0},{6,2},{8,12},{10,14},{12,8},{14,10},{1,5},{3,7},... | collective-permute-start | bytes 110600 | tf_op jit(solution)/shard_map/ppermute | solution.py:30
  22.9 7.2 %collective-permute-start.11 = (bf16[144,128]{1,0:T(8,128)(2,1)S(1)}, bf16[144,128]{1,0:T(8,128)(2,1)S(1)}, u32[]{:S(2)}, u32[]{:S(2)}) collective-permute-start(bf16[144,128]{1,0:T(8,128)(2,1)S(1)} %add_up.7.own), channel_id=1, source_target_pairs={{0,12},{2,14},{4,8},{6,10},{8,4},{10,6},{12,0},{14,2},{1,13},{3,15... | collective-permute-start | bytes 110600 | tf_op jit(solution)/shard_map/ppermute | solution.py:30
  26.7 4.9 %collective-permute-start.12 = (bf16[144,128]{1,0:T(8,128)(2,1)S(1)}, bf16[144,128]{1,0:T(8,128)(2,1)S(1)}, u32[]{:S(2)}, u32[]{:S(2)}) collective-permute-start(bf16[144,128]{1,0:T(8,128)(2,1)S(1)} %add_up.7.own), channel_id=1, source_target_pairs={{0,8},{2,10},{4,12},{6,14},{8,0},{10,2},{12,4},{14,6},{1,9},{3,11}... | collective-permute-start | bytes 110600 | tf_op jit(solution)/shard_map/ppermute | solution.py:30
  26.7 4.9 %collective-permute-start.13 = (bf16[144,128]{1,0:T(8,128)(2,1)S(1)}, bf16[144,128]{1,0:T(8,128)(2,1)S(1)}, u32[]{:S(2)}, u32[]{:S(2)}) collective-permute-start(bf16[144,128]{1,0:T(8,128)(2,1)S(1)} %add_up.7.own), channel_id=1, source_target_pairs={{0,4},{2,6},{4,0},{6,2},{8,12},{10,14},{12,8},{14,10},{1,5},{3,7},... | collective-permute-start | bytes 110600 | tf_op jit(solution)/shard_map/ppermute | solution.py:30
  27.7 5.6 %collective-permute-start.15 = (bf16[576,128]{1,0:T(8,128)(2,1)S(1)}, bf16[576,128]{1,0:T(8,128)(2,1)S(1)}, u32[]{:S(2)}, u32[]{:S(2)}) collective-permute-start(bf16[576,128]{1,0:T(8,128)(2,1)S(1)} %join.2.refs_0_), channel_id=1, source_target_pairs={{0,2},{2,0},{4,6},{6,4},{8,10},{10,8},{12,14},{14,12},{1,3},{3,1},... | collective-permute-start | bytes 442376 | tf_op jit(solution)/shard_map/ppermute | solution.py:30
  31.6 5.2 %collective-permute-start.14 = (bf16[576,128]{1,0:T(8,128)(2,1)S(1)}, bf16[576,128]{1,0:T(8,128)(2,1)S(1)}, u32[]{:S(2)}, u32[]{:S(2)}) collective-permute-start(bf16[576,128]{1,0:T(8,128)(2,1)S(1)} %join.3.refs_0_), channel_id=1, source_target_pairs={{0,2},{2,0},{4,6},{6,4},{8,10},{10,8},{12,14},{14,12},{1,3},{3,1},... | collective-permute-start | bytes 442376 | tf_op jit(solution)/shard_map/ppermute | solution.py:30
  47.3 1.3 %collective-permute-start.16 = (f32[1,8192]{1,0:T(1,128)S(1)}, f32[1,8192]{1,0:T(1,128)S(1)}, u32[]{:S(2)}, u32[]{:S(2)}) collective-permute-start(f32[1,8192]{1,0:T(1,128)S(1)} %sampled.1), channel_id=1, source_target_pairs={{0,1},{1,0},{2,3},{3,2},{4,5},{5,4},{6,7},{7,6},{8,9},{9,8},{10,11... | collective-permute-start | bytes 98312 | tf_op jit(solution)/shard_map/ppermute | solution.py:30
  48.6 3.4 %collective-permute-start.17 = (f32[1,8192]{1,0:T(1,128)S(1)}, f32[1,8192]{1,0:T(1,128)S(1)}, u32[]{:S(2)}, u32[]{:S(2)}) collective-permute-start(f32[1,8192]{1,0:T(1,128)S(1)} %add.12), channel_id=1, source_target_pairs={{0,3},{1,2},{2,1},{3,0},{4,7},{5,6},{6,5},{7,4},{8,11},{9,10},{10,... | collective-permute-start | bytes 98312 | tf_op jit(solution)/shard_map/ppermute | solution.py:259
  52.1 3.4 %collective-permute-start.18 = (f32[1,8192]{1,0:T(1,128)S(1)}, f32[1,8192]{1,0:T(1,128)S(1)}, u32[]{:S(2)}, u32[]{:S(2)}) collective-permute-start(f32[1,8192]{1,0:T(1,128)S(1)} %add.13), channel_id=1, source_target_pairs={{0,5},{1,4},{2,7},{3,6},{4,1},{5,0},{6,3},{7,2},{8,13},{9,12},{10,... | collective-permute-start | bytes 98312 | tf_op jit(solution)/shard_map/ppermute | solution.py:259
  55.5 4.9 %collective-permute-start.19 = (f32[1,8192]{1,0:T(1,128)S(1)}, f32[1,8192]{1,0:T(1,128)S(1)}, u32[]{:S(2)}, u32[]{:S(2)}) collective-permute-start(f32[1,8192]{1,0:T(1,128)S(1)} %add.14), channel_id=1, source_target_pairs={{0,9},{1,8},{2,11},{3,10},{4,13},{5,12},{6,15},{7,14},{8,1},{9,0},... | collective-permute-start | bytes 98312 | tf_op jit(solution)/shard_map/ppermute | solution.py:259
